TPU v7x, 256 devices: a whole 4x4x8 slice. The times are simulated.
256 devices in a mesh: gx: 8 (over z_lo, x), gy: 4 (over y), gz: 8 (over z_hi, core).
Axes of the slice: x: 4, y: 4, z: 8 (z_hi: 4, z_lo: 2; z = z_hi * 2 + z_lo), core: 2. Of those that a mesh axis runs over, the one named last changes fastest.
Arguments:
- orbitals: float32 [96, 48, 128, 256], P('gx', 'gy', 'gz'), may hold values from -6 to 6
- potential: float32 [96, 48, 128], P('gx', 'gy', 'gz'), may hold values from -2 to 0.5
- eig_blocks: float32 [65536, 256], P(('gx', 'gy', 'gz')), may hold values from -0.375 to 0.375
- owners: int32 [2], replicated, may hold values from 0 to 255
- block_ids: int32 [2], replicated, may hold values from 0 to 7
Outputs:
- filtered: float32 [96, 48, 128, 64], P('gx', 'gy', 'gz')
All inputs are finite; a program needn't handle non-finite values.
Results may differ from a plain program's by a relative error of at most 0.00012.
Values sent between devices are 32-bit elements; how exact they have to be, the bound alone decides.
A program may use at most 192 MiB of HBM per device.

v0:
```python
import jax
import jax.numpy as jnp
from jax import lax
from jax.sharding import PartitionSpec as P

PCOL = 32


coef_list = (8.0 / 5.0, -1.0 / 5.0, 8.0 / 315.0, -1.0 / 560.0)
coef_zero = -205.0 / 72.0
center = 5.5
half = 5.0


def extended(array, sides, width):
    for axis, dim in sides:
        devices, length = (lax.axis_size(axis), array.shape[dim])
        up = [(i, (i + 1) % devices) for i in range(devices)]
        down = [(j, i) for i, j in up]
        last = lax.slice_in_dim(array, length - width, length, axis=dim)
        leading = lax.slice_in_dim(array, 0, width, axis=dim)
        before = lax.ppermute(last, axis, up)
        after = lax.ppermute(leading, axis, down)
        array = jnp.concatenate([before, array, after], axis=dim)
    return array


def from_root(block, axis, source):
    block = jnp.where(lax.axis_index(axis) == source, block, jnp.zeros_like(block))
    return lax.psum(block, axis)


def shifted(padded, axis, offset):
    starts = [4, 4, 4, 0]
    limits = [padded.shape[0] - 4, padded.shape[1] - 4, padded.shape[2] - 4, padded.shape[3]]
    starts[axis] = starts[axis] + offset
    limits[axis] = limits[axis] + offset
    return lax.slice(padded, starts, limits)


def apply_inner(padded, pot_region):
    middle = shifted(padded, 0, 0)
    lap = 3.0 * coef_zero * middle
    for axis in range(3):
        for offset in range(4):
            shift = offset + 1
            lap = lap + coef_list[offset] * (
                shifted(padded, axis, shift) + shifted(padded, axis, -shift)
            )
    return -0.5 * lap + pot_region[..., None] * middle


def apply_local(field, potential):
    padded = extended(field, (("gx", 0), ("gy", 1), ("gz", 2)), 4)
    return apply_inner(padded, potential)


def per_device(orbitals, potential, eig_blocks, owners, block_ids):
    states = eig_blocks.shape[1]
    pcol = PCOL
    mine_list = []
    for which in range(2):
        start = block_ids[which] * pcol
        mine_list.append(lax.dynamic_slice_in_dim(eig_blocks, start, pcol, 1))
    panel_list = []
    for which in range(2):
        panel_list.append(from_root(mine_list[which], ("gx", "gy", "gz"), owners[which]))
    rotation = jnp.concatenate(panel_list, axis=1)
    shape = orbitals.shape
    psi = jnp.dot(
        orbitals.reshape(-1, states),
        rotation,
        precision=lax.Precision.HIGHEST,
        preferred_element_type=jnp.float32,
    ).reshape(shape[0], shape[1], shape[2], 2 * pcol)
    first = (apply_local(psi, potential) - center * psi) / half
    second = 2.0 * (apply_local(first, potential) - center * first) / half - psi
    filtered = 2.0 * (apply_local(second, potential) - center * second) / half - first
    return filtered


def solution(mesh):
    placed = (P("gx", "gy", "gz", None), P("gx", "gy", "gz"), P(("gx", "gy", "gz"), None), P(), P())
    return jax.shard_map(
        per_device, mesh=mesh, in_specs=placed, out_specs=P("gx", "gy", "gz", None), check_vma=False
    )
```

profile of v0, /device:TPU:1, one launch (start us, length us, event | category | flops | bytes accessed | tf_op | source)
XLA Modules:
  0.0 484.0 jit_solution(12588924869170636162)
XLA Ops:
  13.8 253.2 %all-reduce.3.cloned.1.call-done = (f32[256,32]{1,0:T(8,128)}, f32[256,32]{1,0:T(8,128)}) async-done(((f32[256,32]{1,0:T(8,128)}, f32[256,32]{1,0:T(8,128)}), (f32[256,32]{1,0:T(8,128)}, f32[256,32]{1,0:T(8,128)})) %all-reduce.3.cloned.1.call-update) | async-done | bytes 65552 | tf_op jit(solution)/shard_map/psum | solution.py:30
  267.1 3.4 convolution_bitcast_fusion
  273.2 3.7 collective-permute-start
  278.3 7.7 %collective-permute-done = f32[4,12,16,64]{3,2,1,0:T(8,128)} collective-permute-done((f32[4,12,16,64]{3,2,1,0:T(8,128)}, f32[4,12,16,64]{3,2,1,0:T(8,128)}, u32[]{:S(2)}, u32[]{:S(2)}) %collective-permute-start) | collective-permute-done | bytes 196640 | tf_op jit(solution)/shard_map/ppermute | solution.py:23
  286.0 4.1 collective-permute-done.1
  291.4 2.7 collective-permute-start.2
  294.1 14.1 %collective-permute-done.3 = f32[20,4,16,64]{3,2,1,0:T(8,128)S(1)} collective-permute-done((f32[20,4,16,64]{3,2,1,0:T(8,128)S(1)}, f32[20,4,16,64]{3,2,1,0:T(8,128)S(1)}, u32[]{:S(2)}, u32[]{:S(2)}) %collective-permute-start.3) | collective-permute-done | bytes 327712 | tf_op jit(solution)/shard_map/ppermute | solution.py:22
  311.9 2.8 collective-permute-start.5
  314.7 3.9 pad_maximum_fusion
  318.7 13.2 %collective-permute-done.4 = f32[20,20,4,64]{3,2,1,0:T(4,128)S(1)} collective-permute-done((f32[20,20,4,64]{3,2,1,0:T(4,128)S(1)}, f32[20,20,4,64]{3,2,1,0:T(4,128)S(1)}, u32[]{:S(2)}, u32[]{:S(2)}) %collective-permute-start.4) | collective-permute-done | bytes 409632 | tf_op jit(solution)/shard_map/ppermute | solution.py:23
  333.7 10.2 %broadcast_multiply_fusion = (f32[12,12,16,64]{3,2,1,0:T(8,128)}, f32[12,12,16,64]{3,2,1,0:T(8,128)}) fusion(f32[12,12,16,64]{3,2,1,0:T(8,128)S(1)} %bitcast.15, f32[12,12,16]{2,1,0:T(8,128)} %param.6, f32[20,4,16,64]{3,2,1,0:T(8,128)} %copy-done.11, f32[4,12,16,64]{3,2,1,0:T(8,128)} %collective-permute-done, f32[4,12,16,64]{3,2,1,0:T(8,128)} %collective-permute-done.1, ...), kind=kLoop, calls=%fused_computation.240 | loop fusion | flops 13418496 | bytes 8365056 | tf_op jit(solution)/shard_map/div | solution.py:76
  345.5 3.6 collective-permute-start.6
  349.0 7.8 %collective-permute-done.7 = f32[4,12,16,64]{3,2,1,0:T(8,128)S(1)} collective-permute-done((f32[4,12,16,64]{3,2,1,0:T(8,128)S(1)}, f32[4,12,16,64]{3,2,1,0:T(8,128)S(1)}, u32[]{:S(2)}, u32[]{:S(2)}) %collective-permute-start.7) | collective-permute-done | bytes 196640 | tf_op jit(solution)/shard_map/ppermute | solution.py:22
  358.6 2.4 collective-permute-start.8
  361.0 13.6 %collective-permute-done.9 = f32[20,4,16,64]{3,2,1,0:T(8,128)S(1)} collective-permute-done((f32[20,4,16,64]{3,2,1,0:T(8,128)S(1)}, f32[20,4,16,64]{3,2,1,0:T(8,128)S(1)}, u32[]{:S(2)}, u32[]{:S(2)}) %collective-permute-start.9) | collective-permute-done | bytes 327712 | tf_op jit(solution)/shard_map/ppermute | solution.py:22
  379.5 2.6 pad_maximum_fusion.1
  382.2 12.7 %collective-permute-done.10 = f32[20,20,4,64]{3,2,1,0:T(4,128)S(1)} collective-permute-done((f32[20,20,4,64]{3,2,1,0:T(4,128)S(1)}, f32[20,20,4,64]{3,2,1,0:T(4,128)S(1)}, u32[]{:S(2)}, u32[]{:S(2)}) %collective-permute-start.10) | collective-permute-done | bytes 409632 | tf_op jit(solution)/shard_map/ppermute | solution.py:23
  396.7 15.4 %multiply_subtract_fusion.1 = f32[12,12,16,64]{3,2,1,0:T(8,128)} fusion(f32[12,12,16,64]{3,2,1,0:T(8,128)S(1)} %bitcast.16, f32[12,12,16,64]{3,2,1,0:T(8,128)} %get-tuple-element.8, f32[20,4,16,64]{3,2,1,0:T(8,128)} %copy-done.10, f32[4,12,16,64]{3,2,1,0:T(8,128)} %copy-done.5, f32[12,12,16,64]{3,2,1,0:T(8,128)} %get-tuple-element.7, ...), kind=kLoop, calls=%fused_computation.215 | loop fusion | flops 13565952 | bytes 8954880 | tf_op jit(solution)/shard_map/sub | solution.py:77
  414.2 2.9 collective-permute-start.12
  417.1 8.9 %collective-permute-done.13 = f32[4,12,16,64]{3,2,1,0:T(8,128)S(1)} collective-permute-done((f32[4,12,16,64]{3,2,1,0:T(8,128)S(1)}, f32[4,12,16,64]{3,2,1,0:T(8,128)S(1)}, u32[]{:S(2)}, u32[]{:S(2)}) %collective-permute-start.13) | collective-permute-done | bytes 196640 | tf_op jit(solution)/shard_map/ppermute | solution.py:22
  428.9 14.6 %collective-permute-done.15 = f32[20,4,16,64]{3,2,1,0:T(8,128)S(1)} collective-permute-done((f32[20,4,16,64]{3,2,1,0:T(8,128)S(1)}, f32[20,4,16,64]{3,2,1,0:T(8,128)S(1)}, u32[]{:S(2)}, u32[]{:S(2)}) %collective-permute-start.15) | collective-permute-done | bytes 327712 | tf_op jit(solution)/shard_map/ppermute | solution.py:22
  446.8 2.7 pad_maximum_fusion.2
  449.5 15.5 %collective-permute-done.16 = f32[20,20,4,64]{3,2,1,0:T(4,128)S(1)} collective-permute-done((f32[20,20,4,64]{3,2,1,0:T(4,128)S(1)}, f32[20,20,4,64]{3,2,1,0:T(4,128)S(1)}, u32[]{:S(2)}, u32[]{:S(2)}) %collective-permute-start.16) | collective-permute-done | bytes 409632 | tf_op jit(solution)/shard_map/ppermute | solution.py:23
  466.9 10.3 %multiply_subtract_fusion = f32[12,12,16,64]{3,2,1,0:T(8,128)} fusion(f32[12,12,16,64]{3,2,1,0:T(8,128)S(1)} %copy-done.2, f32[20,4,16,64]{3,2,1,0:T(8,128)} %copy-done.12, f32[4,12,16,64]{3,2,1,0:T(8,128)} %copy-done.6, f32[4,12,16,64]{3,2,1,0:T(8,128)} %copy-done.4, f32[20,4,16,64]{3,2,1,0:T(8,128)} %copy-done.9, f32[20,20,4,64]{3,2,1,0:T(4,128)} %copy-done.20, ...), kind=kLoop, calls=%fused_computation.214 | loop fusion | flops 13713408 | bytes 8365056 | tf_op jit(solution)/shard_map/sub | solution.py:78
  (80 shorter events, 35.7 us)
Async XLA Ops:
  6.5 260.5 %copy-start = (f32[12,12,16,256]{3,2,1,0:T(8,128)S(1)}, f32[12,12,16,256]{3,2,1,0:T(8,128)}, u32[]{:S(2)}) copy-start(f32[12,12,16,256]{3,2,1,0:T(8,128)} %param.5) | copy-start | bytes 7077892
  6.5 260.5 %all-reduce.3.cloned.1.call-start = ((), (), s32[]{:S(2)}) async-start(), calls=%async_computation | async-start | bytes 524288 | tf_op jit(solution)/shard_map/psum | solution.py:30
  273.2 12.8 %collective-permute-start = (f32[4,12,16,64]{3,2,1,0:T(8,128)}, f32[4,12,16,64]{3,2,1,0:T(8,128)}, u32[]{:S(2)}, u32[]{:S(2)}) collective-permute-start(f32[4,12,16,64]{3,2,1,0:T(8,128)} %bitcast.7), channel_id=1, source_target_pairs={{32,0},{64,32},{96,64},{128,96},{160,128},{192,160},{224,192},{0,2... | collective-permute-start | bytes 589832 | tf_op jit(solution)/shard_map/ppermute | solution.py:23
  276.9 13.2 %collective-permute-start.1 = (f32[4,12,16,64]{3,2,1,0:T(8,128)}, f32[4,12,16,64]{3,2,1,0:T(8,128)}, u32[]{:S(2)}, u32[]{:S(2)}) collective-permute-start(f32[4,12,16,64]{3,2,1,0:T(8,128)} %bitcast.8), channel_id=1, source_target_pairs={{0,32},{32,64},{64,96},{96,128},{128,160},{160,192},{192,224},{224... | collective-permute-start | bytes 589832 | tf_op jit(solution)/shard_map/ppermute | solution.py:22
  291.3 16.8 %collective-permute-start.3 = (f32[20,4,16,64]{3,2,1,0:T(8,128)S(1)}, f32[20,4,16,64]{3,2,1,0:T(8,128)S(1)}, u32[]{:S(2)}, u32[]{:S(2)}) collective-permute-start(f32[20,4,16,64]{3,2,1,0:T(8,128)S(1)} %get-tuple-element.25), channel_id=1, source_target_pairs={{0,8},{8,16},{16,24},{24,0},{1,9},{9,17},{17,25},{25,1},{2,10},{10... | collective-permute-start | bytes 983048 | tf_op jit(solution)/shard_map/ppermute | solution.py:22
  291.4 16.8 %collective-permute-start.2 = (f32[20,4,16,64]{3,2,1,0:T(8,128)S(1)}, f32[20,4,16,64]{3,2,1,0:T(8,128)S(1)}, u32[]{:S(2)}, u32[]{:S(2)}) collective-permute-start(f32[20,4,16,64]{3,2,1,0:T(8,128)S(1)} %get-tuple-element.26), channel_id=1, source_target_pairs={{8,0},{16,8},{24,16},{0,24},{9,1},{17,9},{25,17},{1,25},{10,2},{18... | collective-permute-start | bytes 983048 | tf_op jit(solution)/shard_map/ppermute | solution.py:23
  310.2 21.6 %collective-permute-start.4 = (f32[20,20,4,64]{3,2,1,0:T(4,128)S(1)}, f32[20,20,4,64]{3,2,1,0:T(4,128)S(1)}, u32[]{:S(2)}, u32[]{:S(2)}) collective-permute-start(f32[20,20,4,64]{3,2,1,0:T(4,128)S(1)} %get-tuple-element.13), channel_id=1, source_target_pairs={{1,0},{2,1},{3,2},{4,3},{5,4},{6,5},{7,6},{0,7},{9,8},{10,9},{11,1... | collective-permute-start | bytes 1228808 | tf_op jit(solution)/shard_map/ppermute | solution.py:23
  311.9 20.6 %collective-permute-start.5 = (f32[20,20,4,64]{3,2,1,0:T(4,128)S(1)}, f32[20,20,4,64]{3,2,1,0:T(4,128)S(1)}, u32[]{:S(2)}, u32[]{:S(2)}) collective-permute-start(f32[20,20,4,64]{3,2,1,0:T(4,128)S(1)} %get-tuple-element.14), channel_id=1, source_target_pairs={{0,1},{1,2},{2,3},{3,4},{4,5},{5,6},{6,7},{7,0},{8,9},{9,10},{10,1... | collective-permute-start | bytes 1228808 | tf_op jit(solution)/shard_map/ppermute | solution.py:22
  345.2 11.7 %collective-permute-start.7 = (f32[4,12,16,64]{3,2,1,0:T(8,128)S(1)}, f32[4,12,16,64]{3,2,1,0:T(8,128)S(1)}, u32[]{:S(2)}, u32[]{:S(2)}) collective-permute-start(f32[4,12,16,64]{3,2,1,0:T(8,128)S(1)} %get-tuple-element.29), channel_id=1, source_target_pairs={{0,32},{32,64},{64,96},{96,128},{128,160},{160,192},{192,224},{224... | collective-permute-start | bytes 589832 | tf_op jit(solution)/shard_map/ppermute | solution.py:22
  345.5 11.4 %collective-permute-start.6 = (f32[4,12,16,64]{3,2,1,0:T(8,128)S(1)}, f32[4,12,16,64]{3,2,1,0:T(8,128)S(1)}, u32[]{:S(2)}, u32[]{:S(2)}) collective-permute-start(f32[4,12,16,64]{3,2,1,0:T(8,128)S(1)} %get-tuple-element.30), channel_id=1, source_target_pairs={{32,0},{64,32},{96,64},{128,96},{160,128},{192,160},{224,192},{0,2... | collective-permute-start | bytes 589832 | tf_op jit(solution)/shard_map/ppermute | solution.py:23
  356.8 22.7 %copy-start.3 = (f32[4,12,16,64]{3,2,1,0:T(8,128)}, f32[4,12,16,64]{3,2,1,0:T(8,128)S(1)}, u32[]{:S(2)}) copy-start(f32[4,12,16,64]{3,2,1,0:T(8,128)S(1)} %collective-permute-done.7) | copy-start | bytes 589828
  356.8 22.7 %copy-start.5 = (f32[4,12,16,64]{3,2,1,0:T(8,128)}, f32[4,12,16,64]{3,2,1,0:T(8,128)S(1)}, u32[]{:S(2)}) copy-start(f32[4,12,16,64]{3,2,1,0:T(8,128)S(1)} %collective-permute-done.6) | copy-start | bytes 589828
  357.0 17.7 %collective-permute-start.9 = (f32[20,4,16,64]{3,2,1,0:T(8,128)S(1)}, f32[20,4,16,64]{3,2,1,0:T(8,128)S(1)}, u32[]{:S(2)}, u32[]{:S(2)}) collective-permute-start(f32[20,4,16,64]{3,2,1,0:T(8,128)S(1)} %get-tuple-element.21), channel_id=1, source_target_pairs={{0,8},{8,16},{16,24},{24,0},{1,9},{9,17},{17,25},{25,1},{2,10},{10... | collective-permute-start | bytes 983048 | tf_op jit(solution)/shard_map/ppermute | solution.py:22
  358.6 16.1 %collective-permute-start.8 = (f32[20,4,16,64]{3,2,1,0:T(8,128)S(1)}, f32[20,4,16,64]{3,2,1,0:T(8,128)S(1)}, u32[]{:S(2)}, u32[]{:S(2)}) collective-permute-start(f32[20,4,16,64]{3,2,1,0:T(8,128)S(1)} %get-tuple-element.22), channel_id=1, source_target_pairs={{8,0},{16,8},{24,16},{0,24},{9,1},{17,9},{25,17},{1,25},{10,2},{18... | collective-permute-start | bytes 983048 | tf_op jit(solution)/shard_map/ppermute | solution.py:23
  375.0 19.8 %collective-permute-start.10 = (f32[20,20,4,64]{3,2,1,0:T(4,128)S(1)}, f32[20,20,4,64]{3,2,1,0:T(4,128)S(1)}, u32[]{:S(2)}, u32[]{:S(2)}) collective-permute-start(f32[20,20,4,64]{3,2,1,0:T(4,128)S(1)} %get-tuple-element.11), channel_id=1, source_target_pairs={{1,0},{2,1},{3,2},{4,3},{5,4},{6,5},{7,6},{0,7},{9,8},{10,9},{11,1... | collective-permute-start | bytes 1228808 | tf_op jit(solution)/shard_map/ppermute | solution.py:23
  377.1 17.8 %collective-permute-start.11 = (f32[20,20,4,64]{3,2,1,0:T(4,128)S(1)}, f32[20,20,4,64]{3,2,1,0:T(4,128)S(1)}, u32[]{:S(2)}, u32[]{:S(2)}) collective-permute-start(f32[20,20,4,64]{3,2,1,0:T(4,128)S(1)} %get-tuple-element.12), channel_id=1, source_target_pairs={{0,1},{1,2},{2,3},{3,4},{4,5},{5,6},{6,7},{7,0},{8,9},{9,10},{10,1... | collective-permute-start | bytes 1228808 | tf_op jit(solution)/shard_map/ppermute | solution.py:22
  413.4 12.5 %collective-permute-start.13 = (f32[4,12,16,64]{3,2,1,0:T(8,128)S(1)}, f32[4,12,16,64]{3,2,1,0:T(8,128)S(1)}, u32[]{:S(2)}, u32[]{:S(2)}) collective-permute-start(f32[4,12,16,64]{3,2,1,0:T(8,128)S(1)} %get-tuple-element.27), channel_id=1, source_target_pairs={{0,32},{32,64},{64,96},{96,128},{128,160},{160,192},{192,224},{224... | collective-permute-start | bytes 589832 | tf_op jit(solution)/shard_map/ppermute | solution.py:22
  414.2 11.8 %collective-permute-start.12 = (f32[4,12,16,64]{3,2,1,0:T(8,128)S(1)}, f32[4,12,16,64]{3,2,1,0:T(8,128)S(1)}, u32[]{:S(2)}, u32[]{:S(2)}) collective-permute-start(f32[4,12,16,64]{3,2,1,0:T(8,128)S(1)} %get-tuple-element.28), channel_id=1, source_target_pairs={{32,0},{64,32},{96,64},{128,96},{160,128},{192,160},{224,192},{0,2... | collective-permute-start | bytes 589832 | tf_op jit(solution)/shard_map/ppermute | solution.py:23
  426.0 20.8 %copy-start.4 = (f32[4,12,16,64]{3,2,1,0:T(8,128)}, f32[4,12,16,64]{3,2,1,0:T(8,128)S(1)}, u32[]{:S(2)}) copy-start(f32[4,12,16,64]{3,2,1,0:T(8,128)S(1)} %collective-permute-done.13) | copy-start | bytes 589828
  426.0 20.8 %copy-start.6 = (f32[4,12,16,64]{3,2,1,0:T(8,128)}, f32[4,12,16,64]{3,2,1,0:T(8,128)S(1)}, u32[]{:S(2)}) copy-start(f32[4,12,16,64]{3,2,1,0:T(8,128)S(1)} %collective-permute-done.12) | copy-start | bytes 589828
  426.1 17.4 %collective-permute-start.15 = (f32[20,4,16,64]{3,2,1,0:T(8,128)S(1)}, f32[20,4,16,64]{3,2,1,0:T(8,128)S(1)}, u32[]{:S(2)}, u32[]{:S(2)}) collective-permute-start(f32[20,4,16,64]{3,2,1,0:T(8,128)S(1)} %get-tuple-element.17), channel_id=1, source_target_pairs={{0,8},{8,16},{16,24},{24,0},{1,9},{9,17},{17,25},{25,1},{2,10},{10... | collective-permute-start | bytes 983048 | tf_op jit(solution)/shard_map/ppermute | solution.py:22
  426.8 16.7 %collective-permute-start.14 = (f32[20,4,16,64]{3,2,1,0:T(8,128)S(1)}, f32[20,4,16,64]{3,2,1,0:T(8,128)S(1)}, u32[]{:S(2)}, u32[]{:S(2)}) collective-permute-start(f32[20,4,16,64]{3,2,1,0:T(8,128)S(1)} %get-tuple-element.18), channel_id=1, source_target_pairs={{8,0},{16,8},{24,16},{0,24},{9,1},{17,9},{25,17},{1,25},{10,2},{18... | collective-permute-start | bytes 983048 | tf_op jit(solution)/shard_map/ppermute | solution.py:23
  443.8 21.2 %collective-permute-start.16 = (f32[20,20,4,64]{3,2,1,0:T(4,128)S(1)}, f32[20,20,4,64]{3,2,1,0:T(4,128)S(1)}, u32[]{:S(2)}, u32[]{:S(2)}) collective-permute-start(f32[20,20,4,64]{3,2,1,0:T(4,128)S(1)} %get-tuple-element.9), channel_id=1, source_target_pairs={{1,0},{2,1},{3,2},{4,3},{5,4},{6,5},{7,6},{0,7},{9,8},{10,9},{11,1... | collective-permute-start | bytes 1228808 | tf_op jit(solution)/shard_map/ppermute | solution.py:23
  445.2 19.8 %collective-permute-start.17 = (f32[20,20,4,64]{3,2,1,0:T(4,128)S(1)}, f32[20,20,4,64]{3,2,1,0:T(4,128)S(1)}, u32[]{:S(2)}, u32[]{:S(2)}) collective-permute-start(f32[20,20,4,64]{3,2,1,0:T(4,128)S(1)} %get-tuple-element.10), channel_id=1, source_target_pairs={{0,1},{1,2},{2,3},{3,4},{4,5},{5,6},{6,7},{7,0},{8,9},{9,10},{10,1... | collective-permute-start | bytes 1228808 | tf_op jit(solution)/shard_map/ppermute | solution.py:22
  (16 other events, 82.9 us)
Sparse Core Ops, SparseCore 0:
  13.9 253.0 all-reduce.2
where the time goes:
time: 485 us; the launch traced here: 484 us
  waiting for transfers between devices  366 us (75%)
  other arithmetic  51.8 us (11%)
  starting transfers between devices  32 us (7%)
  between operations  16.2 us (3%)
  local copies, waits for them, and re-layouts  14.5 us (3%)
    psum x1, waiting for transfers between devices, from_root(): return lax.psum(block, axis)  253 us
    ppermute x9, waiting for transfers between devices, extended(): before = lax.ppermute(last, axis, up)  63.8 us
    ppermute x9, waiting for transfers between devices, extended(): after = lax.ppermute(leading, axis, down)  49.1 us
    ppermute x9, starting transfers between devices, extended(): after = lax.ppermute(leading, axis, down)  22.4 us
    sub x1, other arithmetic, per_device(): second = 2.0 * (apply_local(first, potential) - center * first) / half - psi  15.4 us
    concatenate x6, other arithmetic, extended(): array = jnp.concatenate([before, array, after], axis=dim)  10.7 us
    sub x1, other arithmetic, per_device(): 2.0 * (apply_local(second, potential) - center * second) / half - first  10.3 us
    div x1, other arithmetic, per_device(): first = (apply_local(psi, potential) - center * psi) / half  10.2 us
  transfers between devices with their start and end apart: 19, of which 12 were waited for; matrix products, arithmetic and copies ran while one was open for 2% of the time, Pallas kernels for 0%

commit v1 on v0

v1 whole, which is shorter than its diff:
```python
import jax
import jax.numpy as jnp
from jax import lax
from jax.experimental import pallas as pl
from jax.experimental.pallas import tpu as pltpu
from jax.sharding import PartitionSpec as P

MESH = pl.DeviceIdType.MESH
PCOL = 32
coef_list = (8.0 / 5.0, -1.0 / 5.0, 8.0 / 315.0, -1.0 / 560.0)
coef_zero = -205.0 / 72.0
center = 5.5
half = 5.0
SLABS = (0, 8, 4)


def kernel(own_ref, bid_ref, orb_ref, pot_ref, eig_ref, out_ref,
           orb, eig, contrib, r1, r2, full, e0, e1, e2, diag, zs, zr, ohi, olo, w,
           load_sem, g_send, g_recv, h_send, h_recv):
    gx, gy, gz = lax.axis_index("gx"), lax.axis_index("gy"), lax.axis_index("gz")
    x = lax.rem(gx, 4)
    zlo = lax.div(gx, 4)
    fields = (e0, e1, e2)

    plane = []
    line = []
    for k in range(1, 16):
        px, py = lax.rem(x + k // 4, 4), lax.rem(gy + k % 4, 4)
        plane.append((k, px * 4 + py, (zlo * 4 + px, py, gz)))
        pz, pc = lax.rem(zlo + k // 8, 2), lax.rem(gz + k % 8, 8)
        line.append((k, (pz * 4 + x, gy, pc)))
    me = x * 4 + gy
    xup, xdown = (lax.rem(gx + 1, 8), gy, gz), (lax.rem(gx + 7, 8), gy, gz)
    yup, ydown = (gx, lax.rem(gy + 1, 4), gz), (gx, lax.rem(gy + 3, 4), gz)
    zup, zdown = (gx, gy, lax.rem(gz + 1, 8)), (gx, gy, lax.rem(gz + 7, 8))

    barrier = pltpu.get_barrier_semaphore()
    peers = [p for _, _, p in plane] + [p for _, p in line] + [xup, xdown]
    for p in peers:
        pl.semaphore_signal(barrier, inc=1, device_id=p, device_id_type=MESH)

    load_eig = pltpu.make_async_copy(eig_ref, eig, load_sem.at[0])
    load_eig.start()
    load_orb = pltpu.make_async_copy(orb_ref, orb, load_sem.at[1])
    load_orb.start()

    load_eig.wait()
    my_id = (gx * 4 + gy) * 8 + gz
    lane = lax.broadcasted_iota(jnp.int32, (256, 128), 1)
    row = lax.broadcasted_iota(jnp.int32, (256, 128), 0)
    state = lax.rem(lane, 64)
    first = state < PCOL
    owner = jnp.where(first, own_ref[0], own_ref[1])
    column = jnp.where(first, bid_ref[0], bid_ref[1]) * PCOL + lax.rem(state, PCOL)
    pick = jnp.where((row == column) & (owner == my_id), 1.0, 0.0)
    top = jnp.dot(eig[0:128], jnp.where(lane < 64, pick, 0.0), precision=lax.Precision.HIGHEST,
                  preferred_element_type=jnp.float32)
    low = jnp.dot(eig[128:256], jnp.where(lane < 64, 0.0, pick), precision=lax.Precision.HIGHEST,
                  preferred_element_type=jnp.float32)
    contrib[...] = (top + low).reshape(16, 8, 128)
    r1[0] = contrib[me]

    pl.semaphore_wait(barrier, len(peers))

    for k, j, dev in plane:
        pltpu.make_async_remote_copy(src_ref=contrib.at[j], dst_ref=r1.at[k], send_sem=g_send.at[0], recv_sem=g_recv.at[0],
                                     device_id=dev, device_id_type=MESH).start()

    load_orb.wait()

    def split(i, carry):
        for zh in range(2):
            o = orb[i, :, pl.ds(8 * zh, 8), :].reshape(96, 256)
            hi = o.astype(jnp.bfloat16)
            rows = pl.ds(pl.multiple_of(i * 96, 96), 96)
            ohi[zh, rows, :] = hi
            olo[zh, rows, :] = (o - hi.astype(jnp.float32)).astype(jnp.bfloat16)
        return carry

    lax.fori_loop(0, 12, split, 0)

    zmask = lax.broadcasted_iota(jnp.int32, (12, 8, 16), 1) == lax.rem(lax.broadcasted_iota(jnp.int32, (12, 8, 16), 2), 8)
    spread = jnp.where(lax.div(lax.broadcasted_iota(jnp.int32, (16, 128), 0), 8)
                       == lax.div(lax.broadcasted_iota(jnp.int32, (16, 128), 1), 64), 1.0, 0.0)

    def diagonal(i, carry):
        v = (pot_ref[i] - center) / half - 0.3 * coef_zero
        a = jnp.where(zmask, jnp.broadcast_to(v[:, None, :], (12, 8, 16)), 0.0).reshape(96, 16)
        diag[i] = jnp.dot(a, spread, precision=lax.Precision.HIGHEST,
                          preferred_element_type=jnp.float32).reshape(12, 8, 128)
        return carry

    lax.fori_loop(0, 12, diagonal, 0)

    def all_arrived(n, buf):
        return pltpu.make_async_remote_copy(src_ref=buf.at[pl.ds(1, 15)], dst_ref=buf.at[pl.ds(1, 15)], send_sem=g_send.at[n],
                                            recv_sem=g_recv.at[n], device_id=xup, device_id_type=MESH)

    all_arrived(0, r1).wait_recv()
    r2[0] = jnp.sum(r1[...], axis=0)
    for k, dev in line:
        pltpu.make_async_remote_copy(src_ref=r2.at[0], dst_ref=r2.at[k], send_sem=g_send.at[1], recv_sem=g_recv.at[1],
                                     device_id=dev, device_id_type=MESH).start()
    all_arrived(1, r2).wait_recv()
    full[me] = jnp.sum(r2[...], axis=0)
    for k, j, dev in plane:
        pltpu.make_async_remote_copy(src_ref=full.at[me], dst_ref=full.at[me], send_sem=g_send.at[2], recv_sem=g_recv.at[2],
                                     device_id=dev, device_id_type=MESH).start()
    all_arrived(2, full).wait_recv()

    rot = full[...].reshape(128, 128)
    swapped = pltpu.roll(rot, 64, 1)
    lane = lax.broadcasted_iota(jnp.int32, (128, 128), 1)
    for zh in range(2):
        keep = (lane < 64) if zh == 0 else (lane >= 64)
        for kh in range(2):
            part = jnp.where(keep, rot if zh == kh else swapped, 0.0)
            hi = part.astype(jnp.bfloat16)
            w[zh, pl.ds(128 * kh, 128), 0:128] = hi
            w[zh, pl.ds(128 * kh, 128), 128:256] = (part - hi.astype(jnp.float32)).astype(jnp.bfloat16)

    sub = lax.broadcasted_iota(jnp.int32, (8, 128), 0)
    cross = (sub < 4) == (lax.broadcasted_iota(jnp.int32, (8, 128), 1) >= 64)

    def halo(stage, slab=None):
        e = fields[stage]
        out = []

        def add(n, src, dst, dev):
            out.append(pltpu.make_async_remote_copy(src_ref=src, dst_ref=dst, send_sem=h_send.at[stage, n],
                                                    recv_sem=h_recv.at[stage, n], device_id=dev, device_id_type=MESH))

        inner = pl.ds(4, 12)
        for s, x0 in enumerate(SLABS):
            if slab is not None and s != slab:
                continue
            if x0 == 8:
                add(0, e.at[pl.ds(12, 4), inner], e.at[pl.ds(0, 4), inner], xup)
            if x0 == 0:
                add(1, e.at[pl.ds(4, 4), inner], e.at[pl.ds(16, 4), inner], xdown)
            layers = pl.ds(x0, 4)
            add(2 + s, zs.at[stage, layers, :, pl.ds(4, 4)], zr.at[stage, layers, :, pl.ds(4, 4)], zup)
            add(5 + s, zs.at[stage, layers, :, pl.ds(0, 4)], zr.at[stage, layers, :, pl.ds(0, 4)], zdown)
            layers = pl.ds(x0 + 4, 4)
            add(8 + s, e.at[layers, pl.ds(12, 4)], e.at[layers, pl.ds(0, 4)], yup)
            add(11 + s, e.at[layers, pl.ds(4, 4)], e.at[layers, pl.ds(16, 4)], ydown)
        return out

    def pack(stage, i, values):
        for y in range(6):
            zs[stage, i, y] = jnp.where(cross, pltpu.roll(values[y], 64, 1), values[y + 6])

    for s, x0 in enumerate(SLABS):
        rows = pl.ds(x0 * 96, 384)
        acc = jnp.dot(ohi[0, rows, :], w[0], preferred_element_type=jnp.float32)
        acc = acc + jnp.dot(ohi[1, rows, :], w[1], preferred_element_type=jnp.float32)
        psi = acc[:, 0:128] + acc[:, 128:256]
        psi = psi + jnp.dot(olo[0, rows, :], w[0, :, 0:128], preferred_element_type=jnp.float32)
        psi = psi + jnp.dot(olo[1, rows, :], w[1, :, 0:128], preferred_element_type=jnp.float32)
        e0[pl.ds(4 + x0, 4), pl.ds(4, 12)] = psi.reshape(4, 12, 8, 128)

        def pack_layer(i, carry):
            pack(0, i, [e0[i + 4, y + 4] for y in range(12)])
            return carry

        lax.fori_loop(x0, x0 + 4, pack_layer, 0)
        for cp in halo(0, s):
            cp.start()

    for stage in range(3):
        e = fields[stage]
        factor = 1.0 if stage == 0 else 2.0
        weights = [-0.1 * factor * c for c in coef_list]
        for cp in halo(stage):
            cp.wait_recv()

        def layer(i, carry):
            values = []
            column = [e[i + 4, y] for y in range(20)]
            for y in range(12):
                c = column[y + 4]
                rolled = pltpu.roll(c, 64, 1)
                beyond = zr[stage, i, y % 6]
                if y >= 6:
                    beyond = pltpu.roll(beyond, 64, 1)
                beyond = jnp.where(cross, beyond, rolled)
                total = factor * diag[i, y] * c
                for m in range(1, 5):
                    up = pltpu.roll(jnp.where(sub < m, beyond, c), 8 - m, 0)
                    down = pltpu.roll(jnp.where(sub >= 8 - m, beyond, c), m, 0)
                    near = (up + down) + (column[y + 4 + m] + column[y + 4 - m]) + (e[i + 4 + m, y + 4] + e[i + 4 - m, y + 4])
                    total = total + weights[m - 1] * near
                if stage > 0:
                    total = total - fields[stage - 1][i + 4, y + 4]
                if stage < 2:
                    fields[stage + 1][i + 4, y + 4] = total
                    values.append(total)
                else:
                    out_ref[i, y, 0:8, :] = total[:, 0:64]
                    out_ref[i, y, 8:16, :] = pltpu.roll(total, 64, 1)[:, 0:64]
            if stage < 2:
                pack(stage + 1, i, values)
            return carry

        for s, x0 in enumerate(SLABS):
            lax.fori_loop(x0, x0 + 4, layer, 0)
            if stage < 2:
                for cp in halo(stage + 1, s):
                    cp.start()

    for n, buf in enumerate((r1, r2, full)):
        all_arrived(n, buf).wait_send()
    for stage in range(3):
        for cp in halo(stage):
            cp.wait_send()


def per_device(orbitals, potential, eig_blocks, owners, block_ids):
    smem = pl.BlockSpec(memory_space=pltpu.SMEM)
    vmem = pl.BlockSpec(memory_space=pltpu.VMEM)
    hbm = pl.BlockSpec(memory_space=pl.ANY)
    f32, bf16 = jnp.float32, jnp.bfloat16
    scratch = [
        pltpu.VMEM((12, 12, 16, 256), f32),
        pltpu.VMEM((256, 256), f32),
        pltpu.VMEM((16, 8, 128), f32),
        pltpu.VMEM((16, 8, 128), f32),
        pltpu.VMEM((16, 8, 128), f32),
        pltpu.VMEM((16, 8, 128), f32),
        pltpu.VMEM((20, 20, 8, 128), f32),
        pltpu.VMEM((20, 20, 8, 128), f32),
        pltpu.VMEM((20, 20, 8, 128), f32),
        pltpu.VMEM((12, 12, 8, 128), f32),
        pltpu.VMEM((3, 12, 6, 8, 128), f32),
        pltpu.VMEM((3, 12, 6, 8, 128), f32),
        pltpu.VMEM((2, 1152, 256), bf16),
        pltpu.VMEM((2, 1152, 256), bf16),
        pltpu.VMEM((2, 256, 256), bf16),
        pltpu.SemaphoreType.DMA((2,)),
        pltpu.SemaphoreType.DMA((3,)),
        pltpu.SemaphoreType.DMA((3,)),
        pltpu.SemaphoreType.DMA((3, 14)),
        pltpu.SemaphoreType.DMA((3, 14)),
    ]
    return pl.pallas_call(
        kernel,
        out_shape=jax.ShapeDtypeStruct((12, 12, 16, 64), f32),
        in_specs=[smem, smem, hbm, vmem, hbm],
        out_specs=vmem,
        scratch_shapes=scratch,
        compiler_params=pltpu.CompilerParams(
            collective_id=0, has_side_effects=True, vmem_limit_bytes=56 * 2**20
        ),
        name="rotate_filter",
    )(owners, block_ids, orbitals, potential, eig_blocks)


def solution(mesh):
    placed = (P("gx", "gy", "gz", None), P("gx", "gy", "gz"), P(("gx", "gy", "gz"), None), P(), P())
    return jax.shard_map(
        per_device, mesh=mesh, in_specs=placed, out_specs=P("gx", "gy", "gz", None), check_vma=False
    )
```

time: 485 us -> 63.1 us (0.13)
  waiting for transfers between devices: 366 us -> 0 us
  Pallas kernels: 0 us -> 60.5 us
  other arithmetic: 51.8 us -> 0 us
  starting transfers between devices: 32 us -> 0 us
  between operations: 16.2 us -> 0.01 us
  local copies, waits for them, and re-layouts: 14.5 us -> 2.36 us
    psum x1 -> x0, waiting for transfers between devices: 253 us -> none  [from_root(): return lax.psum(block, axis)]
    ppermute x18 -> x0, waiting for transfers between devices: 113 us -> none  [the longest x9 63.8 us: extended(): before = lax.ppermute(last, axis, up)]
    pallas_call x0 -> x1, Pallas kernels: none -> 60.5 us  [per_device(): pl.pallas_call(kernel, out_shape=jax.ShapeDtypeStruct((12, 12, 16, 64), f...]
    ppermute x18 -> x0, starting transfers between devices: 32 us -> none  [the longest x9 22.4 us: extended(): after = lax.ppermute(leading, axis, down)]
    sub x2 -> x0, other arithmetic: 25.7 us -> none  [the longest x1 15.4 us: per_device(): second = 2.0 * (apply_local(first, potential) - center * first) / half - psi]
    concatenate x6 -> x0, other arithmetic: 10.7 us -> none  [extended(): array = jnp.concatenate([before, array, after], axis=dim)]
    div x1 -> x0, other arithmetic: 10.2 us -> none  [per_device(): first = (apply_local(psi, potential) - center * psi) / half]
    slice x7 -> x0, local copies, waits for them, and re-layouts: 7.23 us -> none  [the longest x4 3.49 us: extended(): last = lax.slice_in_dim(array, length - width, length, axis=dim)]
  transfers between devices with their start and end apart: 19 -> 0, of which waited for: 12 -> 0; matrix products, arithmetic and copies ran while one was open for 2% -> 0% of each run, Pallas kernels for 0% -> 0%
where the time goes in v1:
time: 63.1 us; the launch traced here: 62.9 us
  Pallas kernels  60.5 us (96%)
  local copies, waits for them, and re-layouts  2.36 us (4%)
    pallas_call x1, Pallas kernels, per_device(): pl.pallas_call(kernel, out_shape=jax.ShapeDtypeStruct((12, 12, 16, 64), f...  60.5 us
    unnamed x1, local copies, waits for them, and re-layouts  2.36 us

profile of v1, /device:TPU:1, one launch (start us, length us, event | category | flops | bytes accessed | tf_op | source)
XLA Modules:
  0.0 62.9 jit_solution(2644166988008648307)
XLA Ops:
  0.0 60.5 %rotate_filter.1 = f32[12,12,16,64]{3,2,1,0:T(8,128)} custom-call(s32[2]{0:T(128)} %own_ref.1, s32[2]{0:T(128)} %bid_ref.1, f32[12,12,16,256]{3,2,1,0:T(8,128)} %orb_ref.1, f32[12,12,16]{2,1,0:T(8,128)} %pot_ref.1, f32[256,256]{1,0:T(8,128)} %eig_ref.1), custom_call_target="tpu_custom_call" | custom-call | tf_op jit(solution)/shard_map/rotate_filter/pallas_call | solution.py:245
  60.5 2.4 %copy.7 = f32[12,12,16,64]{3,2,1,0:T(8,128)} copy(f32[12,12,16,64]{3,2,1,0:T(8,128)} %rotate_filter.1) | data formatting | bytes 1179648

commit v2 on v1

v2 whole, which is shorter than its diff:
```python
import jax
import jax.numpy as jnp
from jax import lax
from jax.experimental import pallas as pl
from jax.experimental.pallas import tpu as pltpu
from jax.sharding import PartitionSpec as P

MESH = pl.DeviceIdType.MESH
PCOL = 32
coef_list = (8.0 / 5.0, -1.0 / 5.0, 8.0 / 315.0, -1.0 / 560.0)
coef_zero = -205.0 / 72.0
center = 5.5
half = 5.0


def kernel(own_hbm, bid_hbm, orb_ref, pot_hbm, eig_ref, out_ref,
           own_ref, bid_ref, pot_ref, orb, eig, contrib, r1, r2, full, e, diag, xs, xr, zs, zr, done, ohi, olo, w,
           load_sem, g_send, g_recv, h_send, h_recv):
    gx, gy, gz = lax.axis_index("gx"), lax.axis_index("gy"), lax.axis_index("gz")
    x = lax.rem(gx, 4)
    zlo = lax.div(gx, 4)

    loads = []
    for n, (src, dst) in enumerate(((own_hbm, own_ref), (bid_hbm, bid_ref), (eig_ref, eig), (orb_ref, orb), (pot_hbm, pot_ref))):
        loads.append(pltpu.make_async_copy(src, dst, load_sem.at[n]))
        loads[n].start()

    plane = []
    line = []
    for k in range(1, 16):
        px, py = lax.rem(x + k // 4, 4), lax.rem(gy + k % 4, 4)
        plane.append((k, px * 4 + py, (zlo * 4 + px, py, gz)))
        pz, pc = lax.rem(zlo + k // 8, 2), lax.rem(gz + k % 8, 8)
        line.append((k, (pz * 4 + x, gy, pc)))
    me = x * 4 + gy
    xup, xdown = (lax.rem(gx + 1, 8), gy, gz), (lax.rem(gx + 7, 8), gy, gz)
    yup, ydown = (gx, lax.rem(gy + 1, 4), gz), (gx, lax.rem(gy + 3, 4), gz)
    zup, zdown = (gx, gy, lax.rem(gz + 1, 8)), (gx, gy, lax.rem(gz + 7, 8))

    barrier = pltpu.get_barrier_semaphore()
    peers = [p for _, _, p in plane] + [p for _, p in line] + [xup, xdown]
    for p in peers:
        pl.semaphore_signal(barrier, inc=1, device_id=p, device_id_type=MESH)

    for n in range(3):
        loads[n].wait()
    my_id = (gx * 4 + gy) * 8 + gz
    lane = lax.broadcasted_iota(jnp.int32, (256, 128), 1)
    row = lax.broadcasted_iota(jnp.int32, (256, 128), 0)
    state = lax.rem(lane, 64)
    first = state < PCOL
    owner = jnp.where(first, own_ref[0], own_ref[1])
    column = jnp.where(first, bid_ref[0], bid_ref[1]) * PCOL + lax.rem(state, PCOL)
    pick = jnp.where((row == column) & (owner == my_id), 1.0, 0.0)
    top = jnp.dot(eig[0:128], jnp.where(lane < 64, pick, 0.0), precision=lax.Precision.HIGHEST,
                  preferred_element_type=jnp.float32)
    low = jnp.dot(eig[128:256], jnp.where(lane < 64, 0.0, pick), precision=lax.Precision.HIGHEST,
                  preferred_element_type=jnp.float32)
    contrib[...] = (top + low).reshape(16, 8, 128)
    r1[0] = contrib[me]

    pl.semaphore_wait(barrier, len(peers))

    for k, j, dev in plane:
        pltpu.make_async_remote_copy(src_ref=contrib.at[j], dst_ref=r1.at[k], send_sem=g_send.at[0], recv_sem=g_recv.at[0],
                                     device_id=dev, device_id_type=MESH).start()

    loads[3].wait()

    def split(i, carry):
        rows = pl.ds(pl.multiple_of(i * 96, 96), 96)
        for zh in range(2):
            for xh in range(2):
                o = orb[i + 6 * xh, :, pl.ds(8 * zh, 8), :].reshape(96, 256)
                hi = o.astype(jnp.bfloat16)
                columns = pl.ds(256 * (2 * zh + xh), 256)
                ohi[rows, columns] = hi
                olo[rows, columns] = (o - hi.astype(jnp.float32)).astype(jnp.bfloat16)
        return carry

    lax.fori_loop(0, 6, split, 0)

    loads[4].wait()
    zmask = lax.broadcasted_iota(jnp.int32, (12, 8, 16), 1) == lax.rem(lax.broadcasted_iota(jnp.int32, (12, 8, 16), 2), 8)
    zhalf = lax.div(lax.broadcasted_iota(jnp.int32, (16, 128), 0), 8)
    quarter = lax.div(lax.broadcasted_iota(jnp.int32, (16, 128), 1), 32)

    def diagonal(i, carry):
        total = 0.0
        for xh in range(2):
            v = (pot_ref[i + 6 * xh] - center) / half - 0.3 * coef_zero
            a = jnp.where(zmask, jnp.broadcast_to(v[:, None, :], (12, 8, 16)), 0.0).reshape(96, 16)
            spread = jnp.where(quarter == 2 * zhalf + xh, 1.0, 0.0)
            total = total + jnp.dot(a, spread, precision=lax.Precision.HIGHEST, preferred_element_type=jnp.float32)
        diag[i] = total.reshape(12, 8, 128)
        return carry

    lax.fori_loop(0, 6, diagonal, 0)

    def all_arrived(n, buf):
        return pltpu.make_async_remote_copy(src_ref=buf.at[pl.ds(1, 15)], dst_ref=buf.at[pl.ds(1, 15)], send_sem=g_send.at[n],
                                            recv_sem=g_recv.at[n], device_id=xup, device_id_type=MESH)

    all_arrived(0, r1).wait_recv()
    r2[0] = jnp.sum(r1[...], axis=0)
    for k, dev in line:
        pltpu.make_async_remote_copy(src_ref=r2.at[0], dst_ref=r2.at[k], send_sem=g_send.at[1], recv_sem=g_recv.at[1],
                                     device_id=dev, device_id_type=MESH).start()
    all_arrived(1, r2).wait_recv()
    full[me] = jnp.sum(r2[...], axis=0)
    for k, j, dev in plane:
        pltpu.make_async_remote_copy(src_ref=full.at[me], dst_ref=full.at[me], send_sem=g_send.at[2], recv_sem=g_recv.at[2],
                                     device_id=dev, device_id_type=MESH).start()
    all_arrived(2, full).wait_recv()

    sub = lax.broadcasted_iota(jnp.int32, (8, 128), 0)
    lane = lax.broadcasted_iota(jnp.int32, (8, 128), 1)
    cross = (sub < 4) == (lane >= 64)
    lower = lax.rem(lane, 64) < 32
    wide = lax.div(lax.broadcasted_iota(jnp.int32, (128, 128), 1), 32)

    def weights(g):
        rot = full[...].reshape(128, 128)
        rolled = [rot] + [pltpu.roll(rot, 32 * r, 1) for r in range(1, 4)]
        for b in range(4):
            for kh in range(2):
                part = jnp.where(wide == b, rolled[(b - 2 * kh - g) % 4], 0.0)
                hi = part.astype(jnp.bfloat16)
                rows = pl.ds(256 * b + 128 * kh, 128)
                w[g, rows, 0:128] = hi
                w[g, rows, 128:256] = (part - hi.astype(jnp.float32)).astype(jnp.bfloat16)

    def halo(k, g):
        inner = pl.ds(4, 6)
        field = e.at[k, g]
        pairs = (
            (xs.at[k, g, 0], xr.at[k, g, 0], xup),
            (xs.at[k, g, 1], xr.at[k, g, 1], xdown),
            (zs.at[k, g, :, :, pl.ds(4, 4)], zr.at[k, g, :, :, pl.ds(4, 4)], zup),
            (zs.at[k, g, :, :, pl.ds(0, 4)], zr.at[k, g, :, :, pl.ds(0, 4)], zdown),
            (field.at[inner, pl.ds(12, 4)], field.at[inner, pl.ds(0, 4)], yup),
            (field.at[inner, pl.ds(4, 4)], field.at[inner, pl.ds(16, 4)], ydown),
        )
        return [
            pltpu.make_async_remote_copy(src_ref=src, dst_ref=dst, send_sem=h_send.at[k, g, n], recv_sem=h_recv.at[k, g, n],
                                         device_id=dev, device_id_type=MESH)
            for n, (src, dst, dev) in enumerate(pairs)
        ]

    def send(k, g):
        field = e.at[k, g]

        def pack(y, carry):
            for at, side in ((y, 0), (y + 6, 1)):
                c = [field[4 + i, 4 + at] for i in range(6)]
                up = [pltpu.roll(c[i], 32, 1) for i in range(2, 6)]
                down = [pltpu.roll(c[i], 96, 1) for i in range(4)]
                for j in range(2):
                    xs[k, g, 0, j, at] = jnp.where(lower, down[2 + j], c[4 + j])
                    xs[k, g, 1, j, at] = jnp.where(lower, c[j], up[j])
                for i in range(4):
                    field[i, 4 + at] = up[i]
                    field[10 + i, 4 + at] = down[i]
                if side == 0:
                    kept = c
            for i in range(6):
                zs[k, g, i, y] = jnp.where(cross, pltpu.roll(kept[i], 64, 1), c[i])
            return carry

        copies = halo(k, g)
        lax.fori_loop(0, 6, pack, 0, unroll=6)
        for cp in copies:
            cp.start()

    def receive(k, g):
        field = e.at[k, g]
        for cp in halo(k, g):
            cp.wait_recv()

        def unpack(y, carry):
            for j in range(2):
                before, after = xr[k, g, 0, j, y], xr[k, g, 1, j, y]
                field[j, 4 + y] = jnp.where(lower, before, field[j, 4 + y])
                field[2 + j, 4 + y] = jnp.where(lower, pltpu.roll(before, 96, 1), field[2 + j, 4 + y])
                field[10 + j, 4 + y] = jnp.where(lower, field[10 + j, 4 + y], pltpu.roll(after, 32, 1))
                field[12 + j, 4 + y] = jnp.where(lower, field[12 + j, 4 + y], after)
            return carry

        lax.fori_loop(0, 12, unpack, 0, unroll=12)

    def stencil(k, g):
        factor = 1.0 if k == 0 else 2.0
        factors = [-0.1 * factor * c for c in coef_list]
        field = e.at[k, g]

        def layer(i, carry):
            column = [field[i + 4, y] for y in range(20)]
            for y in range(12):
                c = column[y + 4]
                beyond = zr[k, g, i, y % 6]
                if y >= 6:
                    beyond = pltpu.roll(beyond, 64, 1)
                beyond = jnp.where(cross, beyond, pltpu.roll(c, 64, 1))
                total = factor * diag[i, y] * c
                for m in range(1, 5):
                    up = pltpu.roll(jnp.where(sub < m, beyond, c), 8 - m, 0)
                    down = pltpu.roll(jnp.where(sub >= 8 - m, beyond, c), m, 0)
                    near = ((up + down) + (column[y + 4 + m] + column[y + 4 - m])
                            + (field[i + 4 + m, y + 4] + field[i + 4 - m, y + 4]))
                    total = total + factors[m - 1] * near
                if k > 0:
                    total = total - e[k - 1, g, i + 4, y + 4]
                if k < 2:
                    e[k + 1, g, i + 4, y + 4] = total
                elif g == 0:
                    done[i, y] = total
                else:
                    even = jnp.where(lower, done[i, y], pltpu.roll(total, 32, 1))
                    odd = jnp.where(lower, pltpu.roll(done[i, y], 96, 1), total)
                    for xh, v in enumerate((even, odd)):
                        out_ref[i + 6 * xh, y, 0:8, :] = v[:, 0:64]
                        out_ref[i + 6 * xh, y, 8:16, :] = pltpu.roll(v, 64, 1)[:, 0:64]
            return carry

        lax.fori_loop(0, 6, layer, 0, unroll=2)

    for g in range(2):
        weights(g)
        acc = jnp.dot(ohi[...], w[g], preferred_element_type=jnp.float32)
        acc = acc + jnp.dot(olo[...], w[g], preferred_element_type=jnp.float32)
        e[0, g, pl.ds(4, 6), pl.ds(4, 12)] = (acc[:, 0:128] + acc[:, 128:256]).reshape(6, 12, 8, 128)
        send(0, g)

    for k in range(3):
        for g in range(2):
            receive(k, g)
            stencil(k, g)
            if k < 2:
                send(k + 1, g)

    for n, buf in enumerate((r1, r2, full)):
        all_arrived(n, buf).wait_send()
    for k in range(3):
        for g in range(2):
            for cp in halo(k, g):
                cp.wait_send()


def per_device(orbitals, potential, eig_blocks, owners, block_ids):
    hbm = pl.BlockSpec(memory_space=pl.ANY)
    f32, bf16 = jnp.float32, jnp.bfloat16
    scratch = [
        pltpu.SMEM((2,), jnp.int32),
        pltpu.SMEM((2,), jnp.int32),
        pltpu.VMEM((12, 12, 16), f32),
        pltpu.VMEM((12, 12, 16, 256), f32),
        pltpu.VMEM((256, 256), f32),
        pltpu.VMEM((16, 8, 128), f32),
        pltpu.VMEM((16, 8, 128), f32),
        pltpu.VMEM((16, 8, 128), f32),
        pltpu.VMEM((16, 8, 128), f32),
        pltpu.VMEM((3, 2, 14, 20, 8, 128), f32),
        pltpu.VMEM((6, 12, 8, 128), f32),
        pltpu.VMEM((3, 2, 2, 2, 12, 8, 128), f32),
        pltpu.VMEM((3, 2, 2, 2, 12, 8, 128), f32),
        pltpu.VMEM((3, 2, 6, 6, 8, 128), f32),
        pltpu.VMEM((3, 2, 6, 6, 8, 128), f32),
        pltpu.VMEM((6, 12, 8, 128), f32),
        pltpu.VMEM((576, 1024), bf16),
        pltpu.VMEM((576, 1024), bf16),
        pltpu.VMEM((2, 1024, 256), bf16),
        pltpu.SemaphoreType.DMA((5,)),
        pltpu.SemaphoreType.DMA((3,)),
        pltpu.SemaphoreType.DMA((3,)),
        pltpu.SemaphoreType.DMA((3, 2, 6)),
        pltpu.SemaphoreType.DMA((3, 2, 6)),
    ]
    return pl.pallas_call(
        kernel,
        out_shape=pltpu.VMEM((12, 12, 16, 64), f32),
        in_specs=[hbm] * 5,
        out_specs=pl.BlockSpec(memory_space=pltpu.VMEM),
        scratch_shapes=scratch,
        compiler_params=pltpu.CompilerParams(
            collective_id=0, has_side_effects=True, vmem_limit_bytes=56 * 2**20
        ),
        name="rotate_filter",
    )(owners, block_ids, orbitals, potential, eig_blocks)


def solution(mesh):
    placed = (P("gx", "gy", "gz", None), P("gx", "gy", "gz"), P(("gx", "gy", "gz"), None), P(), P())
    return jax.shard_map(
        per_device, mesh=mesh, in_specs=placed, out_specs=P("gx", "gy", "gz", None), check_vma=False
    )
```

time: 63.1 us -> 54.6 us (0.87)
  Pallas kernels: 60.5 us -> 53.5 us
  local copies, waits for them, and re-layouts: 2.36 us -> 1.02 us
    pallas_call x1, Pallas kernels: 60.5 us -> 53.5 us  [per_device(): pl.pallas_call(kernel, out_shape=pltpu.VMEM((12, 12, 16, 64), f32), in_sp...]
    unnamed x1, local copies, waits for them, and re-layouts: 2.36 us -> 1.02 us
where the time goes in v2:
time: 54.6 us
  Pallas kernels  53.5 us (98%)
  local copies, waits for them, and re-layouts  1.02 us (2%)
    pallas_call x1, Pallas kernels, per_device(): pl.pallas_call(kernel, out_shape=pltpu.VMEM((12, 12, 16, 64), f32), in_sp...  53.5 us

profile of v2, /device:TPU:1, one launch (start us, length us, event | category | flops | bytes accessed | tf_op | source)
XLA Modules:
  0.0 54.6 jit_solution(8440423847289120248)
XLA Ops:
  0.0 53.5 %rotate_filter.1 = f32[12,12,16,64]{3,2,1,0:T(8,128)S(1)} custom-call(s32[2]{0:T(128)} %own_hbm.1, s32[2]{0:T(128)} %bid_hbm.1, f32[12,12,16,256]{3,2,1,0:T(8,128)} %orb_ref.1, f32[12,12,16]{2,1,0:T(8,128)} %pot_hbm.1, f32[256,256]{1,0:T(8,128)} %eig_ref.1), custom_call_target="tpu_custom_call" | custom-call | tf_op jit(solution)/shard_map/rotate_filter/pallas_call | solution.py:278
  53.5 1.0 %copy.7 = f32[12,12,16,64]{3,2,1,0:T(8,128)} copy(f32[12,12,16,64]{3,2,1,0:T(8,128)S(1)} %rotate_filter.1) | data formatting | bytes 1179648

commit v3 on v2

--- a/solution.py
+++ b/solution.py
@@ -27,9 +27,10 @@
 
     plane = []
     line = []
-    for k in range(1, 16):
+    for k in sorted(range(1, 16), key=lambda k: -min(k // 4, 4 - k // 4) - min(k % 4, 4 - k % 4)):
         px, py = lax.rem(x + k // 4, 4), lax.rem(gy + k % 4, 4)
         plane.append((k, px * 4 + py, (zlo * 4 + px, py, gz)))
+    for k in sorted(range(1, 16), key=lambda k: -min(k % 8, 8 - k % 8)):
         pz, pc = lax.rem(zlo + k // 8, 2), lax.rem(gz + k % 8, 8)
         line.append((k, (pz * 4 + x, gy, pc)))
     me = x * 4 + gy
@@ -38,7 +39,7 @@
     zup, zdown = (gx, gy, lax.rem(gz + 1, 8)), (gx, gy, lax.rem(gz + 7, 8))
 
     barrier = pltpu.get_barrier_semaphore()
-    peers = [p for _, _, p in plane] + [p for _, p in line] + [xup, xdown]
+    peers = [p for _, _, p in plane] + [p for _, p in line]
     for p in peers:
         pl.semaphore_signal(barrier, inc=1, device_id=p, device_id_type=MESH)
 
@@ -65,6 +66,15 @@
         pltpu.make_async_remote_copy(src_ref=contrib.at[j], dst_ref=r1.at[k], send_sem=g_send.at[0], recv_sem=g_recv.at[0],
                                      device_id=dev, device_id_type=MESH).start()
 
+    def all_arrived(n, buf):
+        return pltpu.make_async_remote_copy(src_ref=buf.at[pl.ds(1, 15)], dst_ref=buf.at[pl.ds(1, 15)], send_sem=g_send.at[n],
+                                            recv_sem=g_recv.at[n], device_id=xup, device_id_type=MESH)
+
+    all_arrived(0, r1).wait_recv()
+    r2[0] = jnp.sum(r1[...], axis=0)
+    for k, dev in line:
+        pltpu.make_async_remote_copy(src_ref=r2.at[0], dst_ref=r2.at[k], send_sem=g_send.at[1], recv_sem=g_recv.at[1],
+                                     device_id=dev, device_id_type=MESH).start()
     loads[3].wait()
 
     def split(i, carry):
@@ -80,6 +90,11 @@
 
     lax.fori_loop(0, 6, split, 0)
 
+    all_arrived(1, r2).wait_recv()
+    full[me] = jnp.sum(r2[...], axis=0)
+    for k, j, dev in plane:
+        pltpu.make_async_remote_copy(src_ref=full.at[me], dst_ref=full.at[me], send_sem=g_send.at[2], recv_sem=g_recv.at[2],
+                                     device_id=dev, device_id_type=MESH).start()
     loads[4].wait()
     zmask = lax.broadcasted_iota(jnp.int32, (12, 8, 16), 1) == lax.rem(lax.broadcasted_iota(jnp.int32, (12, 8, 16), 2), 8)
     zhalf = lax.div(lax.broadcasted_iota(jnp.int32, (16, 128), 0), 8)
@@ -97,20 +112,6 @@
 
     lax.fori_loop(0, 6, diagonal, 0)
 
-    def all_arrived(n, buf):
-        return pltpu.make_async_remote_copy(src_ref=buf.at[pl.ds(1, 15)], dst_ref=buf.at[pl.ds(1, 15)], send_sem=g_send.at[n],
-                                            recv_sem=g_recv.at[n], device_id=xup, device_id_type=MESH)
-
-    all_arrived(0, r1).wait_recv()
-    r2[0] = jnp.sum(r1[...], axis=0)
-    for k, dev in line:
-        pltpu.make_async_remote_copy(src_ref=r2.at[0], dst_ref=r2.at[k], send_sem=g_send.at[1], recv_sem=g_recv.at[1],
-                                     device_id=dev, device_id_type=MESH).start()
-    all_arrived(1, r2).wait_recv()
-    full[me] = jnp.sum(r2[...], axis=0)
-    for k, j, dev in plane:
-        pltpu.make_async_remote_copy(src_ref=full.at[me], dst_ref=full.at[me], send_sem=g_send.at[2], recv_sem=g_recv.at[2],
-                                     device_id=dev, device_id_type=MESH).start()
     all_arrived(2, full).wait_recv()
 
     sub = lax.broadcasted_iota(jnp.int32, (8, 128), 0)
@@ -134,10 +135,10 @@
         inner = pl.ds(4, 6)
         field = e.at[k, g]
         pairs = (
+            (zs.at[k, g, :, :, pl.ds(4, 4)], zr.at[k, g, :, :, pl.ds(4, 4)], zup),
+            (zs.at[k, g, :, :, pl.ds(0, 4)], zr.at[k, g, :, :, pl.ds(0, 4)], zdown),
             (xs.at[k, g, 0], xr.at[k, g, 0], xup),
             (xs.at[k, g, 1], xr.at[k, g, 1], xdown),
-            (zs.at[k, g, :, :, pl.ds(4, 4)], zr.at[k, g, :, :, pl.ds(4, 4)], zup),
-            (zs.at[k, g, :, :, pl.ds(0, 4)], zr.at[k, g, :, :, pl.ds(0, 4)], zdown),
             (field.at[inner, pl.ds(12, 4)], field.at[inner, pl.ds(0, 4)], yup),
             (field.at[inner, pl.ds(4, 4)], field.at[inner, pl.ds(16, 4)], ydown),
         )

time: 54.6 us -> 52.8 us (0.967)
  Pallas kernels: 53.5 us -> 51.5 us
    pallas_call x1, Pallas kernels: 53.5 us -> 51.5 us  [per_device(): pl.pallas_call(kernel, out_shape=pltpu.VMEM((12, 12, 16, 64), f32), in_sp...]
where the time goes in v3:
time: 52.8 us; the launch traced here: 52.6 us
  Pallas kernels  51.5 us (98%)
  local copies, waits for them, and re-layouts  1.02 us (2%)
    pallas_call x1, Pallas kernels, per_device(): pl.pallas_call(kernel, out_shape=pltpu.VMEM((12, 12, 16, 64), f32), in_sp...  51.5 us

profile of v3, /device:TPU:1, one launch (start us, length us, event | category | flops | bytes accessed | tf_op | source)
XLA Modules:
  0.0 52.6 jit_solution(9374280001476623262)
XLA Ops:
  0.0 51.5 %rotate_filter.1 = f32[12,12,16,64]{3,2,1,0:T(8,128)S(1)} custom-call(s32[2]{0:T(128)} %own_hbm.1, s32[2]{0:T(128)} %bid_hbm.1, f32[12,12,16,256]{3,2,1,0:T(8,128)} %orb_ref.1, f32[12,12,16]{2,1,0:T(8,128)} %pot_hbm.1, f32[256,256]{1,0:T(8,128)} %eig_ref.1), custom_call_target="tpu_custom_call" | custom-call | tf_op jit(solution)/shard_map/rotate_filter/pallas_call | solution.py:279
  51.5 1.0 %copy.7 = f32[12,12,16,64]{3,2,1,0:T(8,128)} copy(f32[12,12,16,64]{3,2,1,0:T(8,128)S(1)} %rotate_filter.1) | data formatting | bytes 1179648

commit v4 on v3

--- a/solution.py
+++ b/solution.py
@@ -19,11 +19,6 @@
     gx, gy, gz = lax.axis_index("gx"), lax.axis_index("gy"), lax.axis_index("gz")
     x = lax.rem(gx, 4)
     zlo = lax.div(gx, 4)
-
-    loads = []
-    for n, (src, dst) in enumerate(((own_hbm, own_ref), (bid_hbm, bid_ref), (eig_ref, eig), (orb_ref, orb), (pot_hbm, pot_ref))):
-        loads.append(pltpu.make_async_copy(src, dst, load_sem.at[n]))
-        loads[n].start()
 
     plane = []
     line = []
@@ -40,8 +35,18 @@
 
     barrier = pltpu.get_barrier_semaphore()
     peers = [p for _, _, p in plane] + [p for _, p in line]
-    for p in peers:
+    for p in peers[:15]:
         pl.semaphore_signal(barrier, inc=1, device_id=p, device_id_type=MESH)
+    loads = [
+        pltpu.make_async_copy(src, dst, load_sem.at[n])
+        for n, (src, dst) in enumerate(((own_hbm, own_ref), (bid_hbm, bid_ref), (eig_ref, eig), (orb_ref, orb), (pot_hbm, pot_ref)))
+    ]
+    for n in range(3):
+        loads[n].start()
+    for p in peers[15:]:
+        pl.semaphore_signal(barrier, inc=1, device_id=p, device_id_type=MESH)
+    for n in range(3, 5):
+        loads[n].start()
 
     for n in range(3):
         loads[n].wait()
@@ -204,9 +209,13 @@
                 beyond = jnp.where(cross, beyond, pltpu.roll(c, 64, 1))
                 total = factor * diag[i, y] * c
                 for m in range(1, 5):
-                    up = pltpu.roll(jnp.where(sub < m, beyond, c), 8 - m, 0)
-                    down = pltpu.roll(jnp.where(sub >= 8 - m, beyond, c), m, 0)
-                    near = ((up + down) + (column[y + 4 + m] + column[y + 4 - m])
+                    if m < 4:
+                        up = pltpu.roll(jnp.where(sub < m, beyond, c), 8 - m, 0)
+                        down = pltpu.roll(jnp.where(sub >= 8 - m, beyond, c), m, 0)
+                        along = up + down
+                    else:
+                        along = pltpu.roll(beyond + c, 4, 0)
+                    near = (along + (column[y + 4 + m] + column[y + 4 - m])
                             + (field[i + 4 + m, y + 4] + field[i + 4 - m, y + 4]))
                     total = total + factors[m - 1] * near
                 if k > 0:
@@ -232,19 +241,24 @@
         e[0, g, pl.ds(4, 6), pl.ds(4, 12)] = (acc[:, 0:128] + acc[:, 128:256]).reshape(6, 12, 8, 128)
         send(0, g)
 
+    for n, buf in enumerate((r1, r2, full)):
+        all_arrived(n, buf).wait_send()
+
     for k in range(3):
         for g in range(2):
+            if k > 0:
+                for cp in halo(k - 1, g):
+                    cp.wait_send()
+            if k == 2 and g == 1:
+                for cp in halo(2, 0):
+                    cp.wait_send()
             receive(k, g)
             stencil(k, g)
             if k < 2:
                 send(k + 1, g)
 
-    for n, buf in enumerate((r1, r2, full)):
-        all_arrived(n, buf).wait_send()
-    for k in range(3):
-        for g in range(2):
-            for cp in halo(k, g):
-                cp.wait_send()
+    for cp in halo(2, 1):
+        cp.wait_send()
 
 
 def per_device(orbitals, potential, eig_blocks, owners, block_ids):

time: 52.8 us -> 52.6 us (level)
  no operation moved by 1% of the time
where the time goes in v4:
time: 52.6 us; the launch traced here: 52.5 us
  Pallas kernels  51.4 us (98%)
  local copies, waits for them, and re-layouts  1.02 us (2%)
    pallas_call x1, Pallas kernels, per_device(): pl.pallas_call(kernel, out_shape=pltpu.VMEM((12, 12, 16, 64), f32), in_sp...  51.4 us

profile of v4, /device:TPU:1, one launch (start us, length us, event | category | flops | bytes accessed | tf_op | source)
XLA Modules:
  0.0 52.5 jit_solution(13458340861486309674)
XLA Ops:
  0.0 51.4 %rotate_filter.1 = f32[12,12,16,64]{3,2,1,0:T(8,128)S(1)} custom-call(s32[2]{0:T(128)} %own_hbm.1, s32[2]{0:T(128)} %bid_hbm.1, f32[12,12,16,256]{3,2,1,0:T(8,128)} %orb_ref.1, f32[12,12,16]{2,1,0:T(8,128)} %pot_hbm.1, f32[256,256]{1,0:T(8,128)} %eig_ref.1), custom_call_target="tpu_custom_call" | custom-call | tf_op jit(solution)/shard_map/rotate_filter/pallas_call | solution.py:293
  51.5 1.0 %copy.7 = f32[12,12,16,64]{3,2,1,0:T(8,128)} copy(f32[12,12,16,64]{3,2,1,0:T(8,128)S(1)} %rotate_filter.1) | data formatting | bytes 1179648
